TPU v7x, 256 devices: a whole 4x4x8 slice. The times are simulated.
256 devices in a mesh: expert: 4 (over y_lo, core), tensor: 64 (over x, y_hi, z).
Axes of the slice: x: 4, y: 4 (y_hi: 2, y_lo: 2; y = y_hi * 2 + y_lo), z: 8, core: 2. Of those that a mesh axis runs over, the one named last changes fastest.
Arguments:
- tokens: bfloat16 [1024, 6144], P('expert', 'tensor'), may hold values from -6 to 6
- expert_ids: int32 [1024, 2], P('expert'), may hold values from 0 to 3, all different within a row; in each aligned block of 256 rows (0 to 255, 256 to 511, ...) at most 192 rows name the same one
- route_gates: float32 [1024, 2], P('expert'), may hold values from 0.2 to 1
- w_gate: bfloat16 [4, 6144, 16384], P('expert', None, 'tensor'), may hold values from -0.078125 to 0.078125
- w_up: bfloat16 [4, 6144, 16384], P('expert', None, 'tensor'), may hold values from -0.078125 to 0.078125
- w_down: bfloat16 [4, 16384, 6144], P('expert', 'tensor'), may hold values from -0.125 to 0.125
Outputs:
- mixed: bfloat16 [1024, 6144], P('expert', 'tensor')
Inputs may be any that keep to these rules, and one draw needn't show every extreme that they name: `expert_ids`: each token names two different experts; in each aligned block of 256 tokens no expert is named by more than 192 tokens, a bound that some block reaches.
All inputs are finite; a program needn't handle non-finite values.
Results may differ from a plain program's by a relative error of at most 0.012.
Values may be sent and summed in bfloat16 or wider, within the bound.
No kernel may reach another device: no remote copies, remote signals or barrier semaphores. Data moves between devices by JAX's collectives and lax.ppermute only.
A program may use at most 128 MiB of HBM per device.

v0:
```python
import jax
import jax.numpy as jnp
from jax import lax
from jax.sharding import PartitionSpec as P

CAP = 192


def body(tokens, expert_ids, route_gates, w_gate, w_up, w_down):
    tok_rows = tokens.shape[0]
    groups = lax.axis_size("expert")
    capacity = CAP
    slot_count = groups * capacity
    gate_local = w_gate[0]
    up_local = w_up[0]
    down_local = w_down[0]
    onehot = (expert_ids[:, :, None] == jnp.arange(groups, dtype=jnp.int32)[None, None, :]).astype(
        jnp.int32
    )
    flattened = onehot.reshape(tok_rows * 2, groups)
    earlier = jnp.cumsum(flattened, axis=0) - flattened
    offsets = jnp.arange(groups, dtype=jnp.int32)[None, :] * capacity
    slot_of = jnp.sum(flattened * (earlier + offsets), axis=1).reshape(tok_rows, 2)
    matches = slot_of[:, :, None] == jnp.arange(slot_count, dtype=jnp.int32)[None, None, :]
    placing = jnp.sum(matches.astype(jnp.float32), axis=1).astype(jnp.bfloat16).T
    combine_weights = jnp.sum(matches.astype(jnp.float32) * route_gates[:, :, None], axis=1)
    outgoing = jnp.dot(placing, tokens, preferred_element_type=jnp.float32).astype(jnp.bfloat16)
    arrived = lax.all_to_all(outgoing, "expert", split_axis=0, concat_axis=0, tiled=True)
    piece = lax.all_gather(arrived, "tensor", axis=1, tiled=True)
    gate = jnp.dot(piece, gate_local, preferred_element_type=jnp.float32)
    up_part = jnp.dot(piece, up_local, preferred_element_type=jnp.float32)
    hidden = (jax.nn.silu(gate) * up_part).astype(jnp.bfloat16)
    summed = lax.psum_scatter(
        lax.dot_general(
            down_local, hidden, (((0,), (1,)), ((), ())), preferred_element_type=jnp.float32
        ),
        "tensor",
        scatter_dimension=0,
        tiled=True,
    )
    outcome = summed.astype(jnp.bfloat16)
    back = lax.all_to_all(outcome, "expert", split_axis=1, concat_axis=1, tiled=True)
    mixed = lax.dot_general(combine_weights, back.astype(jnp.float32), (((1,), (1,)), ((), ())))
    return mixed.astype(jnp.bfloat16)


def solution(mesh):
    in_specs = (
        P("expert", "tensor"),
        P("expert", None),
        P("expert", None),
        P("expert", None, "tensor"),
        P("expert", None, "tensor"),
        P("expert", "tensor", None),
    )
    out_specs = P("expert", "tensor")
    return jax.shard_map(body, mesh=mesh, in_specs=in_specs, out_specs=out_specs, check_vma=False)
```

profile of v0, /device:TPU:1, one launch (start us, length us, event | category | flops | bytes accessed | tf_op | source)
XLA Modules:
  0.0 1115.6 jit_solution(5423483404875156522)
XLA Ops:
  6.5 0.0 copy-start
  6.5 0.0 all-gather.2.cloned.1.call-start
  6.5 1.0 copy.20
  7.5 0.1 eq.45
  7.7 0.1 eq.41
  7.8 1.2 reduce-window.6
  9.0 0.2 slice_reduce_fusion
  9.3 0.2 reduce-window.9
  9.4 0.1 add_bitcast_fusion
  9.5 0.1 fusion.23
  9.6 0.1 eq.49
  9.8 0.1 copy.22
  9.8 1.1 convert_reduce_fusion
  10.9 1.7 convolution_convert_fusion
  12.6 1.8 all_to_all.16
  14.4 0.9 copy.23
  15.3 10.2 all_to_all.24
  25.5 0.8 copy.24
  26.3 1.8 all_to_all.18
  28.1 0.0 all-gather.2.cloned.1.call-update
  28.1 0.0 reduce-scatter.4.cloned.1.call-start
  28.2 153.2 %all-gather.2.cloned.1.call-done = bf16[768,6144]{0,1:T(8,128)(2,1)} async-done(((bf16[768,96]{0,1:T(8,128)(2,1)}), bf16[768,6144]{0,1:T(8,128)(2,1)}) %all-gather.2.cloned.1.call-update) | async-done | bytes 9437200 | tf_op jit(solution)/shard_map/all_gather | solution.py:29
  181.4 8.1 fusion.3
  189.5 0.0 copy-done
  189.5 21.1 %convolution_bitcast_fusion = f32[6144,768]{0,1:T(8,128)} fusion(bf16[1,256,6144]{2,1,0:T(8,128)(2,1)S(1)} %copy-done, bf16[768,6144]{0,1:T(8,128)(2,1)} %all-gather.2.cloned.1.call-done, bf16[1,6144,256]{2,1,0:T(8,128)(2,1)} %param.10, f32[768,256]{1,0:T(8,128)} %fusion.3), kind=kOutput, calls=%fused_computation | convolution fusion | flops 4833017856 | bytes 35389440 | tf_op jit(solution)/shard_map/dot_general | solution.py:34
  210.6 18.7 %copy.25 = f32[6144,768]{1,0:T(8,128)} copy(f32[6144,768]{0,1:T(8,128)} %convolution_bitcast_fusion) | data formatting | bytes 37748736
  229.4 0.0 reduce-scatter.4.cloned.1.call-update
  229.4 863.8 %reduce-scatter.4.cloned.1.call-done = f32[96,768]{1,0:T(8,128)} async-done(((f32[6144,768]{1,0:T(8,128)}), f32[96,768]{1,0:T(8,128)}) %reduce-scatter.4.cloned.1.call-update) | async-done | bytes 294928
  1093.1 1.8 copy.26
  1094.9 13.0 %all_to_all.25 = bf16[96,4,192]{0,2,1:T(8,128)(2,1)S(1)} all-to-all(bf16[96,4,192]{0,2,1:T(8,128)(2,1)} %bitcast.54), channel_id=1, replica_groups=mesh['expert'=4,'tensor'=64] {'expert'}, dimensions={1} | all-to-all | bytes 294912 | tf_op jit(solution)/shard_map/all_to_all | solution.py:42
  1107.9 0.9 fusion.26
  (2 shorter events, 0.0 us)
Async XLA Ops:
  6.5 183.0 %copy-start = (bf16[1,256,6144]{2,1,0:T(8,128)(2,1)S(1)}, bf16[1,256,6144]{2,1,0:T(8,128)(2,1)}, u32[]{:S(2)}) copy-start(bf16[1,256,6144]{2,1,0:T(8,128)(2,1)} %param.11) | copy-start | bytes 9437188
  6.5 174.9 %all-gather.2.cloned.1.call-start = ((), (), s32[]{:S(2)}) async-start(), calls=%async_computation.3 | async-start | bytes 9584640 | tf_op jit(solution)/shard_map/all_gather | solution.py:29
  28.1 1065.0 %reduce-scatter.4.cloned.1.call-start = ((), (), s32[]{:S(2)}) async-start(), calls=%async_computation.4 | async-start | bytes 19169280
Sparse Core Ops, SparseCore 0:
  28.3 153.1 all-gather.1
  229.5 863.5 reduce-scatter.3
where the time goes:
time: 1120 us
  waiting for transfers between devices  1020 us (91%)
  matrix products  31.8 us (3%)
  local copies, waits for them, and re-layouts  27.5 us (2%)
  blocking collectives  23.2 us (2%)
  between operations  13.4 us (1%)
    unnamed x3, waiting for transfers between devices  864 us
    all_gather x1, waiting for transfers between devices, body(): piece = lax.all_gather(arrived, 'tensor', axis=1, tiled=True)  153 us
  transfers between devices with their start and end apart: 2, of which 2 were waited for; matrix products, arithmetic and copies ran while one was open for 0% of the time, Pallas kernels for 0%

commit v1 on v0

--- a/solution.py
+++ b/solution.py
@@ -26,7 +26,15 @@
     combine_weights = jnp.sum(matches.astype(jnp.float32) * route_gates[:, :, None], axis=1)
     outgoing = jnp.dot(placing, tokens, preferred_element_type=jnp.float32).astype(jnp.bfloat16)
     arrived = lax.all_to_all(outgoing, "expert", split_axis=0, concat_axis=0, tiled=True)
-    piece = lax.all_gather(arrived, "tensor", axis=1, tiled=True)
+    piece = jnp.concatenate(
+        lax.all_to_all(
+            jnp.stack([arrived] * lax.axis_size("tensor"), axis=0),
+            axis_name="tensor",
+            split_axis=0,
+            concat_axis=0,
+        ),
+        axis=1,
+    )
     gate = jnp.dot(piece, gate_local, preferred_element_type=jnp.float32)
     up_part = jnp.dot(piece, up_local, preferred_element_type=jnp.float32)
     hidden = (jax.nn.silu(gate) * up_part).astype(jnp.bfloat16)

time: 1120 us -> 1180 us (1.054)
  blocking collectives: 23.2 us -> 242 us
  waiting for transfers between devices: 1020 us -> 865 us
    all_to_all x0 -> x1, blocking collectives: none -> 220 us  [body(): lax.all_to_all(jnp.stack([arrived] * lax.axis_size('tensor'), axis=0), ax...]
    all_gather x1 -> x0, waiting for transfers between devices: 153 us -> none  [body(): piece = lax.all_gather(arrived, 'tensor', axis=1, tiled=True)]
    unnamed x5 -> x11, local copies, waits for them, and re-layouts: 21.4 us -> 25.2 us
    unnamed x3 -> x2, waiting for transfers between devices: 864 us -> 865 us
  transfers between devices with their start and end apart: 2 -> 1, of which waited for: 2 -> 1; matrix products, arithmetic and copies ran while one was open for 0% -> 0% of each run, Pallas kernels for 0% -> 0%
where the time goes in v1:
time: 1180 us
  waiting for transfers between devices  865 us (73%)
  blocking collectives  242 us (21%)
  local copies, waits for them, and re-layouts  33.3 us (3%)
  matrix products  27.2 us (2%)
  between operations  13.5 us (1%)
    unnamed x2, waiting for transfers between devices  865 us
    all_to_all x1, blocking collectives, body(): lax.all_to_all(jnp.stack([arrived] * lax.axis_size('tensor'), axis=0), ax...  220 us
    unnamed x11, local copies, waits for them, and re-layouts  25.2 us
  transfers between devices with their start and end apart: 1, of which 1 were waited for; matrix products, arithmetic and copies ran while one was open for 0% of the time, Pallas kernels for 0%

profile of v1, /device:TPU:1, one launch (start us, length us, event | category | flops | bytes accessed | tf_op | source)
XLA Modules:
  0.0 1183.5 jit_solution(11602427868070632741)
XLA Ops:
  6.5 0.0 copy-start
  6.5 1.0 copy.21
  7.5 0.1 eq.45
  7.7 0.1 eq.41
  7.8 1.2 reduce-window.6
  9.0 0.2 slice_reduce_fusion
  9.3 0.2 reduce-window.9
  9.4 0.1 add_bitcast_fusion
  9.5 0.1 fusion.23
  9.6 0.1 eq.49
  9.8 0.1 copy.23
  9.8 1.1 convert_reduce_fusion
  10.9 1.7 convolution_convert_fusion
  12.6 1.8 all_to_all.17
  14.4 0.9 copy.24
  15.3 10.2 all_to_all.26
  25.5 0.8 copy.25
  26.3 1.8 stack.4
  28.1 2.0 stack.5
  30.2 0.0 copy-start.3
  30.2 219.5 %all_to_all.27 = bf16[64,768,96]{1,2,0:T(8,128)(2,1)S(1)} all-to-all(bf16[64,768,96]{1,2,0:T(8,128)(2,1)S(1)} %stack.5), channel_id=1, replica_groups=mesh['expert'=4,'tensor'=64] {'tensor'}, dimensions={0} | all-to-all | bytes 18874368 | tf_op jit(solution)/shard_map/all_to_all | solution.py:30
  249.7 3.7 copy-done.2
  253.4 3.5 fusion.3
  256.9 21.1 %convolution_bitcast_fusion = f32[6144,768]{0,1:T(8,128)} fusion(bf16[1,256,6144]{2,1,0:T(8,128)(2,1)S(1)} %copy-done, bf16[768,6144]{0,1:T(8,128)(2,1)} %bitcast.57, bf16[1,6144,256]{2,1,0:T(8,128)(2,1)} %param.10, f32[768,256]{1,0:T(8,128)} %fusion.3), kind=kOutput, calls=%fused_computation | convolution fusion | flops 4833017856 | bytes 35389440 | tf_op jit(solution)/shard_map/dot_general | solution.py:42
  278.0 18.7 %copy.26 = f32[6144,768]{1,0:T(8,128)} copy(f32[6144,768]{0,1:T(8,128)} %convolution_bitcast_fusion) | data formatting | bytes 37748736
  296.8 0.0 reduce-scatter.4.cloned.1.call-update
  296.8 0.0 copy-start.1
  296.8 864.7 %reduce-scatter.4.cloned.1.call-done = f32[96,768]{1,0:T(8,128)} async-done(((f32[6144,768]{1,0:T(8,128)}), f32[96,768]{1,0:T(8,128)}) %reduce-scatter.4.cloned.1.call-update) | async-done | bytes 294928
  1161.5 1.8 copy.27
  1163.3 12.4 %all_to_all.28 = bf16[96,4,192]{0,2,1:T(8,128)(2,1)S(1)} all-to-all(bf16[96,4,192]{0,2,1:T(8,128)(2,1)} %bitcast.59), channel_id=1, replica_groups=mesh['expert'=4,'tensor'=64] {'expert'}, dimensions={1} | all-to-all | bytes 294912 | tf_op jit(solution)/shard_map/all_to_all | solution.py:50
  1175.7 0.9 fusion.26
  1176.6 0.0 copy-done.1
  (6 shorter events, 0.0 us)
Async XLA Ops:
  6.5 250.4 %copy-start = (bf16[1,256,6144]{2,1,0:T(8,128)(2,1)S(1)}, bf16[1,256,6144]{2,1,0:T(8,128)(2,1)}, u32[]{:S(2)}) copy-start(bf16[1,256,6144]{2,1,0:T(8,128)(2,1)} %param.11) | copy-start | bytes 9437188
  6.5 1155.0 %reduce-scatter.4.cloned.1.call-start = ((), (), s32[]{:S(2)}) async-start(), calls=%async_computation.4 | async-start | bytes 19169280
  30.2 223.3 %copy-start.3 = (bf16[1,6144,256]{2,1,0:T(8,128)(2,1)S(1)}, bf16[1,6144,256]{2,1,0:T(8,128)(2,1)}, u32[]{:S(2)}) copy-start(bf16[1,6144,256]{2,1,0:T(8,128)(2,1)} %param.9) | copy-start | bytes 9437188
  249.7 3.7 copy-start.2
  296.8 879.9 %copy-start.1 = (bf16[1,256,6144]{2,1,0:T(8,128)(2,1)S(1)}, bf16[1,256,6144]{2,1,0:T(8,128)(2,1)}, u32[]{:S(2)}) copy-start(bf16[1,256,6144]{2,1,0:T(8,128)(2,1)} %param.11) | copy-start | bytes 9437188
Sparse Core Ops, SparseCore 0:
  296.9 864.5 reduce-scatter.3
